TPU v7x, 128 devices: a whole 4x4x4 slice. The times are simulated.
128 devices in a mesh: head: 2 (over core), outer: 8 (over z_hi, y), inner: 8 (over z_lo, x).
Axes of the slice: x: 4, y: 4, z: 4 (z_hi: 2, z_lo: 2; z = z_hi * 2 + z_lo), core: 2. Of those that a mesh axis runs over, the one named last changes fastest.
Arguments:
- queries: bfloat16 [8192, 4096], P(('outer', 'inner'), 'head'), may hold values from -17 to 17
- keys: bfloat16 [8192, 1024], P(('outer', 'inner'), 'head'), may hold values from -17 to 17
- values: bfloat16 [8192, 1024], P(('outer', 'inner'), 'head'), may hold values from -6 to 6
- permutation: int32 [128], replicated, may hold values from 0 to 127, each once
- segment: int32 [8192], replicated, may hold values from 0 to 7, never falling along the last dimension, each value on 1 to 2048 neighbouring positions
Outputs:
- attended: bfloat16 [8192, 4096], P(('outer', 'inner'), 'head')
Inputs may be any that keep to these rules, and one draw needn't show every extreme that they name: `permutation`: each of the 128 episode blocks is held by exactly one slot. `segment`: ids never fall along the episode; each id covers 1 to 2048 positions and one covers exactly 2048.
All inputs are finite; a program needn't handle non-finite values.
Results may differ from a plain program's by a relative error of at most 0.0054.
Values may be sent and summed in bfloat16 or wider, within the bound.
A program may use at most 192 MiB of HBM per device.

v0:
```python
import math

import jax
import jax.numpy as jnp
from jax import lax
from jax.experimental import pallas as pl
from jax.experimental.pallas import tpu as pltpu
from jax.sharding import Mesh, PartitionSpec as P

HEAD_DIM = 128
BLOCK = 64
BLOCKS = 128
SEQ = 8192
SEGMENTS = 8
GROUP = 4
RING = 4
LOCAL = 128
ROWS = GROUP * BLOCK
WIDE = GROUP * HEAD_DIM
HELD = 2 * RING
REACH = 34
WIDTH = REACH * BLOCK
SCALE = math.log2(math.e) / math.sqrt(HEAD_DIM)
NEG = -1e30
MESH = pl.DeviceIdType.MESH
AXES = ("head", "z_hi", "y", "z_lo", "x")


def landing(slot):
    z = (slot >> 6) * 2 + ((slot >> 3) & 1)
    y = (slot >> 4) & 3
    return (((slot & 1) * RING + z) * RING + y) * RING + ((slot >> 1) & 3)


def turn(value, shift):
    return (value + shift) & (RING - 1)


def columns(j, width):
    return pl.ds(pl.multiple_of(j * width, width), width)


def tables(perm, seg):
    lane = lax.broadcasted_iota(jnp.int32, (1, BLOCKS), 1)
    starts = jnp.zeros((1, BLOCKS), jnp.int32)
    for s in range(1, SEGMENTS):
        count = jnp.sum((seg < s).astype(jnp.int32), axis=1, keepdims=True)
        count = jnp.sum(count, axis=0, keepdims=True)
        starts = jnp.where(lane == s, count, starts)
    slot = lax.broadcasted_iota(jnp.int32, (BLOCKS, BLOCKS), 0)
    block = lax.broadcasted_iota(jnp.int32, (BLOCKS, BLOCKS), 1)
    held = jnp.sum(jnp.where(slot == block, perm, 0), axis=1, keepdims=True)
    inverse = jnp.sum(jnp.where(held == block, landing(slot), 0), axis=0, keepdims=True)
    inverse = jnp.minimum(inverse, BLOCKS - 1)
    return jnp.concatenate([perm, starts, inverse, jnp.zeros((5, BLOCKS), jnp.int32)], axis=0)


def episode_kernel(
    q_ref, k_ref, v_ref, perm_ref, seg_ref, out_ref,
    perm, seg, meta_vec, meta, q_all, k_all, v_all, k_part, v_part, k_raw, v_raw, weights, scale, o_all,
    send_sem, recv_sem, first_send, first_recv, o_send, o_recv, local_sem,
):
    core, z_hi, y, z_lo, x = (lax.axis_index(a) for a in AXES)
    z = z_hi * 2 + z_lo
    other = 1 - core
    apart = (z_lo + core) & 1
    home = apart == 0
    away = jnp.logical_not(home)
    half = x >> 1
    x_odd, y_odd = x & 1, y & 1

    def cube(b, ex, ey, ez):
        way = 1 - 2 * b
        return ex * way * (1 - 2 * x_odd), ey * way * (1 - 2 * y_odd), ez * way * (1 - 2 * z_lo)

    def at(to_core, dx=0, dy=0, dz=0):
        far_z = turn(z, dz)
        return (to_core, far_z >> 1, turn(y, dy), far_z & 1, turn(x, dx))

    barrier = pltpu.get_barrier_semaphore()

    def tell(device):
        pl.semaphore_signal(barrier, inc=1, device_id=device, device_id_type=MESH)

    own_key = home & (half == core)
    across = [(ex, ey) for ey in range(2) for ex in range(2)]
    for dy in (1, 2, 3):
        tell(at(core, 0, dy))
    for n in range(2):
        for dz in range(RING):
            device = at(z_lo, 2 * core + n - x, 0, dz)
            if dz:
                tell(device)
            else:
                pl.when(jnp.logical_not(home & (x == 2 * core + n)))(lambda device=device: tell(device))
    for ex, ey in across:
        tell(at(z_lo, *cube(core, ex, ey, 1)))
        tell(at(other, *cube(other, ex, ey, apart)))

    def tell_home():
        for ex, ey in across[1:]:
            tell(at(core, *cube(core, ex, ey, 0)))

    def tell_away():
        for ex, ey in across:
            tell(at(z_lo, *cube(core, ex, ey, 0)))
            tell(at(core, *cube(core, ex, ey, 1)))

    pl.when(home)(tell_home)
    pl.when(away)(tell_away)
    early = [
        pltpu.make_async_copy(src, dst, local_sem.at[n])
        for n, (src, dst) in enumerate((
            *(
                (ref.at[1, :, columns(2 * odd + y_odd, HEAD_DIM)], raw.at[y, odd])
                for ref, raw in ((k_ref, k_raw), (v_ref, v_raw))
                for odd in range(2)
            ),
            (perm_ref, perm),
            (seg_ref, seg),
        ))
    ]
    for copy in early:
        copy.start()
    pl.semaphore_wait(barrier, 22 + 5 * apart - own_key.astype(jnp.int32))

    firsts = []

    def first(src, dst, n, device, own=False):
        copy = pltpu.make_async_remote_copy(
            src_ref=src,
            dst_ref=dst,
            send_sem=first_send.at[len(firsts)],
            recv_sem=first_recv.at[n],
            device_id=device,
            device_id_type=MESH,
        )
        firsts.append((copy, own))
        if own is False:
            copy.start()
        else:
            pl.when(jnp.logical_not(own))(copy.start)
            pl.when(own)(pltpu.make_async_copy(src, dst, first_recv.at[n]).start)

    def landed(ref, n):
        pltpu.make_async_copy(ref, ref, first_recv.at[n]).wait()

    def left(copies):
        for copy, own in copies:
            if own is False:
                copy.wait_send()
            else:
                pl.when(jnp.logical_not(own))(copy.wait_send)

    count = [0]

    def send(src, dst, device):
        n = count[0]
        count[0] += 1
        copy = pltpu.make_async_remote_copy(
            src_ref=src,
            dst_ref=dst,
            send_sem=send_sem.at[n],
            recv_sem=recv_sem.at[n],
            device_id=device,
            device_id_type=MESH,
        )
        copy.start()
        return copy

    targets = [(k, dx) for k in range(2) for dx in (1, 3, 2, 0)]
    ways = ((1, -1), (3, 1), (2, 2))
    here_x = pl.ds(2 * core, 2)

    class Spread:
        def __init__(self, ref, part, raw, everything, offset, own_sem):
            self.ref, self.part, self.raw, self.all, self.offset = ref, part, raw, everything, offset
            self.own_sem = own_sem
            self.shares = []

        def straight(self, source, dst, offset):
            before = len(firsts)
            for k, dx in targets:
                first(
                    source(((x + dx) & 1)),
                    dst,
                    self.offset + offset + z * 2 + x_odd,
                    at(half, dx, 0, apart + 2 * k),
                    own_key if k == 0 and dx == 0 else False,
                )
            return firsts[before:]

        def share(self, src, dst):
            self.shares.append(send(src, dst, at(other)))

        def start(self):
            self.out = self.straight(
                lambda odd: self.ref.at[0, :, columns(odd, 2 * HEAD_DIM)], self.part.at[z, x_odd], 0
            )
            self.along = [
                send(
                    self.ref.at[1, :, columns(2 * odd + ((y + d) & 1), HEAD_DIM)],
                    self.raw.at[y, odd],
                    at(core, 0, d),
                )
                for d, _ in ways
                for odd in range(2)
            ]

        def first_lands(self):
            for line in range(RING):
                for odd in range(2):
                    landed(self.part.at[line, odd], self.offset + line * 2 + odd)
            dst = self.all.at[0:RING, y, here_x]

            def piece(d):
                return self.part.at[:, :, :, columns(((y + d) & 1), HEAD_DIM)]

            self.far = [send(piece(d), dst, at(core, 0, d)) for d, _ in ways]
            self.share(piece(0), dst)
            self.own = pltpu.make_async_copy(piece(0), dst, self.own_sem)
            self.own.start()

        def second_lands(self):
            for copy in self.along:
                copy.wait_recv()
            self.second = self.straight(
                lambda odd: self.raw.at[:, odd], self.all.at[RING + z, :, x], 8
            )

        def take_first(self, n):
            self.far[n].wait_recv()
            ref = self.all.at[0:RING, turn(y, ways[n][1]), here_x]
            self.share(ref, ref)

        def take_second(self, dz):
            line = turn(z, dz)
            for odd in range(2):
                landed(self.all.at[RING + line, :, 2 * core + odd], self.offset + 8 + line * 2 + odd)
            ref = self.all.at[RING + line, :, here_x]
            self.share(ref, ref)

    keys = Spread(k_ref, k_part, k_raw, k_all, 0, local_sem.at[7])
    values = Spread(v_ref, v_part, v_raw, v_all, 16, local_sem.at[8])
    keys.start()
    before = len(firsts)
    for b in range(2):
        for ex, ey in reversed(across):
            n = apart * 4 + ey * 2 + ex
            first(
                q_ref.at[b, :, columns(2 * ((x + ex) & 1) + ((y + ey) & 1), WIDE)],
                q_all.at[n],
                32 + n,
                at(b, *cube(b, ex, ey, apart)),
                home & (core == b) if not (ex or ey) else False,
            )
    asked = firsts[before:]
    values.start()
    for copy in early:
        copy.wait()
    meta_vec[...] = tables(perm[...], seg[...])
    to_scalars = pltpu.make_async_copy(meta_vec, meta, local_sem.at[6])
    to_scalars.start()

    keys.second_lands()
    keys.first_lands()
    for copy in keys.far:
        copy.wait_send()
    values.first_lands()
    left(keys.second)
    values.second_lands()
    for n in range(3):
        keys.take_first(n)
    for dz in (0, 1, 3, 2):
        keys.take_second(dz)
    to_scalars.wait()
    for n in range(HELD):
        landed(q_all.at[n], 32 + n)
    keys.own.wait()
    for copy in keys.shares:
        copy.wait_recv()

    def later():
        left(keys.out + values.out + asked)
        for copy in keys.along + values.along + keys.shares:
            copy.wait_send()
        yield
        for n in range(3):
            values.take_first(n)
            yield
        for dz in (0, 1, 3, 2):
            values.take_second(dz)
            yield
        left(values.second)
        for copy in values.far + values.shares:
            copy.wait_send()
        values.own.wait()
        for copy in values.shares:
            copy.wait_recv()
        yield

    v_steps = later()
    next(v_steps)

    def slot(n):
        dx, dy, dz = cube(core, n % 2, n // 2 % 2, n // 4)
        far_z = turn(z, dz)
        return ((((far_z >> 1) * RING + turn(y, dy)) * 2 + (far_z & 1)) * RING + turn(x, dx)) * 2 + core

    def rows_of(ref, block, start, count):
        parts = []
        for u in range(count):
            there = jnp.clip(block - (REACH - 1) + start + u, 0, BLOCKS - 1)
            place = meta[2, there]
            parts.append(ref[place >> 4, (place >> 2) & 3, place & 3])
        return jnp.concatenate(parts, axis=0)

    def score(i):
        block = meta[0, slot(i)]
        row_pos = block * BLOCK + lax.broadcasted_iota(jnp.int32, (BLOCK, HEAD_DIM), 0)
        row_low = jnp.zeros((BLOCK, HEAD_DIM), jnp.int32)
        for s in range(1, SEGMENTS):
            row_low = jnp.where(meta[1, s] <= row_pos, meta[1, s], row_low)
        q = jnp.concatenate(
            [q_all[i, :, j * HEAD_DIM:(j + 1) * HEAD_DIM] for j in range(GROUP)], axis=0
        )
        pieces = []
        top = None
        for start in range(-2, REACH - 2, 4):
            begin, count = max(start, 0), 4 + min(start, 0)
            s = lax.dot_general(
                q, rows_of(k_all, block, begin, count), (((1,), (1,)), ((), ())),
                preferred_element_type=jnp.float32,
            )
            for half in range(count // 2):
                index = begin + 2 * half
                col = (block - (REACH - 1) + index) * BLOCK + lax.broadcasted_iota(
                    jnp.int32, (BLOCK, HEAD_DIM), 1
                )
                seen = col >= row_low
                if index == REACH - 2:
                    seen = seen & (col <= row_pos)
                seen = jnp.concatenate([seen] * GROUP, axis=0)
                piece = jnp.where(seen, s[:, half * HEAD_DIM:(half + 1) * HEAD_DIM], NEG)
                pieces.append(piece)
                top = piece if top is None else jnp.maximum(top, piece)
        top = jnp.max(top, axis=1, keepdims=True)
        total = None
        for n, piece in enumerate(pieces):
            weight = jnp.exp2((piece - top) * SCALE)
            total = weight if total is None else total + weight
            weights[i, :, n * HEAD_DIM:(n + 1) * HEAD_DIM] = weight.astype(jnp.bfloat16)
        total = jnp.sum(total, axis=1, keepdims=True)
        scale[i] = jnp.broadcast_to(1.0 / total, (ROWS, HEAD_DIM))

    for n in range(0, HELD, 4):
        for m in range(n, n + 4):
            score(m)
        for _ in range(4):
            next(v_steps)

    def blend(i):
        block = meta[0, slot(i)]
        mixed = jnp.dot(weights[i], rows_of(v_all, block, 0, REACH), preferred_element_type=jnp.float32)
        return (mixed * scale[i]).astype(jnp.bfloat16)

    def place(ref, mixed):
        for j in range(GROUP):
            ref[:, j * HEAD_DIM:(j + 1) * HEAD_DIM] = mixed[j * BLOCK:(j + 1) * BLOCK]

    rows = pl.ds(pl.multiple_of(core * BLOCK, BLOCK), BLOCK)
    mine = columns(2 * x_odd + y_odd, WIDE)

    def answer(n):
        return pltpu.make_async_remote_copy(
            src_ref=o_all.at[n],
            dst_ref=out_ref.at[rows, mine],
            send_sem=o_send.at[n],
            recv_sem=o_recv.at[core * 4 + n % 4],
            device_id=at(z_lo, *cube(core, n % 2, n // 2 % 2, n // 4)),
            device_id_type=MESH,
        )

    for n in (7, 6, 5, 3, 4, 2, 1, 0):
        mixed = blend(n)
        for j in range(GROUP):
            o_all[n, :, j * HEAD_DIM:(j + 1) * HEAD_DIM] = mixed[j * BLOCK:(j + 1) * BLOCK]
        if n:
            answer(n).start()
    pl.when(away)(answer(0).start)
    pl.when(home)(
        pltpu.make_async_copy(o_all.at[0], out_ref.at[rows, mine], o_recv.at[core * 4]).start
    )
    for b in range(2):
        for n, (ex, ey) in enumerate(across):
            j = 2 * ((x + ex) & 1) + ((y + ey) & 1)
            ref = out_ref.at[b * BLOCK:(b + 1) * BLOCK, columns(j, WIDE)]
            pltpu.make_async_copy(ref, ref, o_recv.at[b * 4 + n]).wait()
    for n in range(1, HELD):
        answer(n).wait_send()
    pl.when(away)(answer(0).wait_send)


COPIES = 2 * (6 + 3 + 8)
FIRSTS = 2 * (8 + 8) + 8


def shards(queries, keys, values, permutation, segment):
    hbm = pl.BlockSpec(memory_space=pltpu.HBM)
    inputs = (
        *(a.reshape(2, BLOCK, -1) for a in (queries, keys, values)),
        permutation.reshape(1, BLOCKS),
        segment.reshape(SEQ // BLOCKS, BLOCKS),
    )
    return pl.pallas_call(
        episode_kernel,
        out_shape=jax.ShapeDtypeStruct(queries.shape, jnp.bfloat16),
        in_specs=[hbm] * 5,
        out_specs=pl.BlockSpec(memory_space=pltpu.VMEM),
        scratch_shapes=[
            pltpu.VMEM((1, BLOCKS), jnp.int32),
            pltpu.VMEM((SEQ // BLOCKS, BLOCKS), jnp.int32),
            pltpu.VMEM((8, BLOCKS), jnp.int32),
            pltpu.SMEM((8, BLOCKS), jnp.int32),
            pltpu.VMEM((HELD, BLOCK, WIDE), jnp.bfloat16),
            pltpu.VMEM((2 * RING, RING, RING, BLOCK, HEAD_DIM), jnp.bfloat16),
            pltpu.VMEM((2 * RING, RING, RING, BLOCK, HEAD_DIM), jnp.bfloat16),
            pltpu.VMEM((RING, 2, BLOCK, 2 * HEAD_DIM), jnp.bfloat16),
            pltpu.VMEM((RING, 2, BLOCK, 2 * HEAD_DIM), jnp.bfloat16),
            pltpu.VMEM((RING, 2, BLOCK, HEAD_DIM), jnp.bfloat16),
            pltpu.VMEM((RING, 2, BLOCK, HEAD_DIM), jnp.bfloat16),
            pltpu.VMEM((HELD, ROWS, WIDTH), jnp.bfloat16),
            pltpu.VMEM((HELD, ROWS, HEAD_DIM), jnp.float32),
            pltpu.VMEM((HELD, BLOCK, WIDE), jnp.bfloat16),
            pltpu.SemaphoreType.DMA((COPIES,)),
            pltpu.SemaphoreType.DMA((COPIES,)),
            pltpu.SemaphoreType.DMA((FIRSTS,)),
            pltpu.SemaphoreType.DMA((FIRSTS,)),
            pltpu.SemaphoreType.DMA((HELD,)),
            pltpu.SemaphoreType.DMA((HELD,)),
            pltpu.SemaphoreType.DMA((9,)),
        ],
        compiler_params=pltpu.CompilerParams(
            collective_id=0, has_side_effects=True, vmem_limit_bytes=40 << 20
        ),
        name="episode",
    )(*(pltpu.with_memory_space_constraint(a, pltpu.HBM) for a in inputs))


def solution(mesh):
    fine = Mesh(mesh.devices.reshape(2, 2, 4, 2, 4), AXES)
    slots = AXES[1:]
    return jax.shard_map(
        shards,
        mesh=fine,
        in_specs=(P(slots, "head"), P(slots, "head"), P(slots, "head"), P(), P()),
        out_specs=P(slots, "head"),
        check_vma=False,
    )
```

profile of v0, /device:TPU:1, one launch (start us, length us, event | category | flops | bytes accessed | tf_op | source)
XLA Modules:
  0.0 45.2 jit_solution(949319382972896749)
XLA Ops:
  0.0 44.4 %episode.1 = bf16[128,2048]{1,0:T(8,128)(2,1)S(1)} custom-call(bf16[2,64,2048]{2,1,0:T(8,128)(2,1)} %bitcast.5, bf16[2,64,512]{2,1,0:T(8,128)(2,1)} %bitcast.6, bf16[2,64,512]{2,1,0:T(8,128)(2,1)} %bitcast.7, s32[1,128]{1,0:T(1,128)} %bitcast.9, s32[64,128]{1,0:T(8,128)} %bitcast.8), custom_call_target="tpu_custom_call" | custom-call | tf_op jit(solution)/shard_map/episode/pallas_call | solution.py:415
  44.4 0.8 %copy.7 = bf16[128,2048]{1,0:T(8,128)(2,1)} copy(bf16[128,2048]{1,0:T(8,128)(2,1)S(1)} %episode.1) | data formatting | bytes 1048576
where the time goes:
time: 45.3 us; the launch traced here: 45.2 us
  Pallas kernels  44.4 us (98%)
  local copies, waits for them, and re-layouts  0.8 us (2%)
    pallas_call x1, Pallas kernels, shards(): pl.pallas_call(episode_kernel, out_shape=jax.ShapeDtypeStruct(queries.sha...  44.4 us

commit v1 on v0

--- a/solution.py
+++ b/solution.py
@@ -194,9 +194,6 @@
             self.shares.append(send(src, dst, at(other)))
 
         def start(self):
-            self.out = self.straight(
-                lambda odd: self.ref.at[0, :, columns(odd, 2 * HEAD_DIM)], self.part.at[z, x_odd], 0
-            )
             self.along = [
                 send(
                     self.ref.at[1, :, columns(2 * odd + ((y + d) & 1), HEAD_DIM)],
@@ -206,6 +203,9 @@
                 for d, _ in ways
                 for odd in range(2)
             ]
+            self.out = self.straight(
+                lambda odd: self.ref.at[0, :, columns(odd, 2 * HEAD_DIM)], self.part.at[z, x_odd], 0
+            )
 
         def first_lands(self):
             for line in range(RING):

time: 45.3 us -> 45.4 us (level)
  no operation moved by 1% of the time
where the time goes in v1:
time: 45.4 us; the launch traced here: 45.3 us
  Pallas kernels  44.4 us (98%)
  local copies, waits for them, and re-layouts  0.8 us (2%)
    pallas_call x1, Pallas kernels, shards(): pl.pallas_call(episode_kernel, out_shape=jax.ShapeDtypeStruct(queries.sha...  44.4 us

profile of v1, /device:TPU:1, one launch (start us, length us, event | category | flops | bytes accessed | tf_op | source)
XLA Modules:
  0.0 45.3 jit_solution(12218286908003634947)
XLA Ops:
  0.0 44.4 %episode.1 = bf16[128,2048]{1,0:T(8,128)(2,1)S(1)} custom-call(bf16[2,64,2048]{2,1,0:T(8,128)(2,1)} %bitcast.5, bf16[2,64,512]{2,1,0:T(8,128)(2,1)} %bitcast.6, bf16[2,64,512]{2,1,0:T(8,128)(2,1)} %bitcast.7, s32[1,128]{1,0:T(1,128)} %bitcast.9, s32[64,128]{1,0:T(8,128)} %bitcast.8), custom_call_target="tpu_custom_call" | custom-call | tf_op jit(solution)/shard_map/episode/pallas_call | solution.py:415
  44.5 0.8 %copy.7 = bf16[128,2048]{1,0:T(8,128)(2,1)} copy(bf16[128,2048]{1,0:T(8,128)(2,1)S(1)} %episode.1) | data formatting | bytes 1048576

commit v2 on v0

--- a/solution.py
+++ b/solution.py
@@ -264,11 +264,11 @@
 
     keys.second_lands()
     keys.first_lands()
+    left(keys.second)
+    values.second_lands()
     for copy in keys.far:
         copy.wait_send()
     values.first_lands()
-    left(keys.second)
-    values.second_lands()
     for n in range(3):
         keys.take_first(n)
     for dz in (0, 1, 3, 2):

time: 45.3 us -> 45.7 us (level)
  no operation moved by 1% of the time
where the time goes in v2:
time: 45.7 us; the launch traced here: 45.6 us
  Pallas kernels  44.8 us (98%)
  local copies, waits for them, and re-layouts  0.8 us (2%)
    pallas_call x1, Pallas kernels, shards(): pl.pallas_call(episode_kernel, out_shape=jax.ShapeDtypeStruct(queries.sha...  44.8 us

profile of v2, /device:TPU:1, one launch (start us, length us, event | category | flops | bytes accessed | tf_op | source)
XLA Modules:
  0.0 45.6 jit_solution(5392882286538596815)
XLA Ops:
  0.0 44.8 %episode.1 = bf16[128,2048]{1,0:T(8,128)(2,1)S(1)} custom-call(bf16[2,64,2048]{2,1,0:T(8,128)(2,1)} %bitcast.5, bf16[2,64,512]{2,1,0:T(8,128)(2,1)} %bitcast.6, bf16[2,64,512]{2,1,0:T(8,128)(2,1)} %bitcast.7, s32[1,128]{1,0:T(1,128)} %bitcast.9, s32[64,128]{1,0:T(8,128)} %bitcast.8), custom_call_target="tpu_custom_call" | custom-call | tf_op jit(solution)/shard_map/episode/pallas_call | solution.py:415
  44.8 0.8 %copy.7 = bf16[128,2048]{1,0:T(8,128)(2,1)} copy(bf16[128,2048]{1,0:T(8,128)(2,1)S(1)} %episode.1) | data formatting | bytes 1048576
